TPU v7x, 256 devices: a whole 4x4x8 slice. The times are simulated.
256 devices in a mesh: pipe: 8 (over z), expert: 32 (over y, x, core).
Axes of the slice: x: 4, y: 4, z: 8, core: 2. Of those that a mesh axis runs over, the one named last changes fastest.
Arguments:
- activations: bfloat16 [2, 2048, 2560], P(None, 'expert'), may hold values from -6 to 6
- norm_gain: bfloat16 [8, 2560], P('pipe'), may hold values from 0.099609375 to 1.8984375
- placement: int32 [8, 32], P('pipe'), may hold values from 0 to 31, each once within a row
- expert_ids: int32 [8, 2, 2048, 6], P('pipe', None, 'expert'), may hold values from 0 to 31, all different within a row; in each aligned block of 32 rows (0 to 31, 32 to 63, ..., all dimensions but the last counted through in order) at most 9 rows name the same one
- expert_weights: float32 [8, 2, 2048, 6], P('pipe', None, 'expert'), may hold values from 0.05 to 0.45
- gate_store: bfloat16 [8, 32, 2560, 768], P('pipe', 'expert'), may hold values from -0.125 to 0.125
- up_store: bfloat16 [8, 32, 2560, 768], P('pipe', 'expert'), may hold values from -0.125 to 0.125
- down_store: bfloat16 [8, 32, 768, 2560], P('pipe', 'expert'), may hold values from -0.21875 to 0.21875
Outputs:
- layer_outputs: bfloat16 [8, 2, 2048, 2560], P('pipe', None, 'expert')
Inputs may be any that keep to these rules, and one draw needn't show every extreme that they name: `expert_ids`: in every aligned block of 32 rows (rows of all leading dimensions taken in order, so a device's 64 tokens of one layer and microbatch are two blocks) no expert is named by more than 9 rows; some expert is named by exactly 9 rows in some block of every draw. A row names 6 different experts. Each row is a permutation: slot s of layer l holds the weights of expert placement[l, s].
All inputs are finite; a program needn't handle non-finite values.
Results may differ from a plain program's by a relative error of at most 0.024.
Values may be sent and summed in bfloat16 or wider, within the bound.
A program may use at most 64 MiB of HBM per device.

v0:
```python
import jax
import jax.numpy as jnp
from jax import lax
from jax.sharding import PartitionSpec as P

epsilon = 1e-06


def passed_along(value, axis, steps):
    count = lax.axis_size(axis)
    leading, last = (max(0, -steps), min(count, count - steps))
    return lax.ppermute(value, axis, [(source, source + steps) for source in range(leading, last)])


def on_device(
    activations, norm_gain, placement, expert_ids, expert_weights, gate_store, up_store, down_store
):
    section_count = lax.axis_size("pipe")
    section_index = lax.axis_index("pipe")
    group_size = lax.axis_size("expert")
    micro_count, tok_local, model_width = activations.shape
    top_count = expert_ids.shape[-1]
    slot_count = placement.shape[1]
    local_experts = gate_store.shape[1]
    half_rows = tok_local // 2
    most_half = min(
        half_rows, max(2, (half_rows * top_count + slot_count - 1) // slot_count * 3 // 2)
    )
    piece_count = micro_count * tok_local // tok_local
    block_count = tok_local // half_rows
    capacity = block_count * most_half
    tick_count = piece_count + section_count - 1
    input_rows = activations.reshape(micro_count * tok_local, model_width)
    route_table = expert_ids.reshape(micro_count * tok_local, top_count)
    weight_table = expert_weights.reshape(micro_count * tok_local, top_count)
    gain_row = norm_gain[0].astype(jnp.float32)
    place_row = placement[0]
    expert_iota = jnp.arange(slot_count, dtype=jnp.int32)
    owner = jnp.sum(
        expert_iota[None, :] * (place_row[None, :] == expert_iota[:, None]).astype(jnp.int32),
        axis=1,
    )
    gate_w = gate_store[0]
    up_w = up_store[0]
    down_w = down_store[0]

    def expert_compute(received):
        gate_value = jnp.einsum(
            "sjrd,jdf->sjrf", received, gate_w, preferred_element_type=jnp.float32
        )
        up_value = jnp.einsum("sjrd,jdf->sjrf", received, up_w, preferred_element_type=jnp.float32)
        hidden = (jax.nn.silu(gate_value) * up_value).astype(jnp.bfloat16)
        return jnp.einsum(
            "sjrf,jfd->sjrd", hidden, down_w, preferred_element_type=jnp.float32
        ).astype(jnp.bfloat16)

    def expert_skip(received):
        return jnp.zeros_like(received)

    def run_piece(piece_input, piece_index, active):
        row_start = piece_index * tok_local
        route_rows = lax.dynamic_slice_in_dim(route_table, row_start, tok_local, 0)
        weight_rows = lax.dynamic_slice_in_dim(weight_table, row_start, tok_local, 0)
        values = piece_input.astype(jnp.float32)
        inverse = lax.rsqrt(jnp.mean(values * values, axis=-1, keepdims=True) + epsilon)
        normed = (values * inverse * gain_row).astype(jnp.bfloat16)
        flat_ids = route_rows.reshape(block_count, half_rows * top_count)
        onehot = (flat_ids[:, :, None] == expert_iota[None, None, :]).astype(jnp.int32)
        before = jnp.cumsum(onehot, axis=1) - onehot
        slot_rank = jnp.sum(before * onehot, axis=-1)
        row_in_slot = slot_rank + jnp.arange(block_count, dtype=jnp.int32)[:, None] * most_half
        slot_of = jnp.sum(onehot * owner[None, None, :], axis=-1)
        target = (slot_of * capacity + row_in_slot).reshape(tok_local * top_count)
        positions = jnp.arange(slot_count * capacity, dtype=jnp.int32)
        matches = positions[:, None] == target[None, :]
        token_of = jnp.arange(tok_local * top_count, dtype=jnp.int32) // top_count
        source = jnp.sum(jnp.where(matches, token_of[None, :], 0), axis=1)
        filled = jnp.any(matches, axis=1) & active
        outgoing = jnp.where(
            filled[:, None], jnp.take(normed, source, axis=0), jnp.zeros((), jnp.bfloat16)
        )
        outgoing = outgoing.reshape(group_size, local_experts, capacity, model_width)
        computed = lax.cond(
            active,
            expert_compute,
            expert_skip,
            lax.all_to_all(outgoing, "expert", split_axis=0, concat_axis=0, tiled=True),
        )
        answers = lax.all_to_all(computed, "expert", split_axis=0, concat_axis=0, tiled=True)
        picked = jnp.take(answers.reshape(slot_count * capacity, model_width), target, axis=0)
        picked = picked.reshape(tok_local, top_count, model_width)
        mixed = jnp.sum(weight_rows[:, :, None] * picked.astype(jnp.float32), axis=1)
        produced = (values + mixed).astype(jnp.bfloat16)
        return jnp.where(active, produced, jnp.zeros_like(produced))

    def tick(tick_index, state_pair):
        incoming, collected = state_pair
        piece_index = tick_index - section_index
        active = (piece_index >= 0) & (piece_index < piece_count)
        clipped = jnp.clip(piece_index, 0, piece_count - 1)
        fresh_rows = lax.dynamic_slice_in_dim(input_rows, clipped * tok_local, tok_local, 0)
        piece_input = jnp.where(section_index == 0, fresh_rows, incoming)
        produced = run_piece(piece_input, clipped, active)
        previous = lax.dynamic_slice_in_dim(collected, clipped * tok_local, tok_local, 0)
        collected = lax.dynamic_update_slice_in_dim(
            collected, jnp.where(active, produced, previous), clipped * tok_local, 0
        )
        incoming = passed_along(produced, "pipe", 1)
        return (incoming, collected)

    initial = (jnp.zeros((tok_local, model_width), jnp.bfloat16), jnp.zeros_like(input_rows))
    final_pair = lax.fori_loop(0, tick_count, tick, initial)
    return final_pair[1].reshape(1, micro_count, tok_local, model_width)


def solution(mesh):
    in_specs = (
        P(None, "expert", None),
        P("pipe", None),
        P("pipe", None),
        P("pipe", None, "expert", None),
        P("pipe", None, "expert", None),
        P("pipe", "expert", None, None),
        P("pipe", "expert", None, None),
        P("pipe", "expert", None, None),
    )
    out_specs = P("pipe", None, "expert", None)
    return jax.shard_map(
        on_device, mesh=mesh, in_specs=in_specs, out_specs=out_specs, check_vma=False
    )
```

profile of v0, /device:TPU:227, one launch (start us, length us, event | category | flops | bytes accessed | tf_op | source)
XLA Modules:
  0.0 1524.3 jit_solution(7133042626027658251)
XLA Ops:
  4.0 1520.3 %while.19 = (s32[]{:T(128)}, bf16[64,2560]{1,0:T(8,128)(2,1)S(1)}, bf16[128,2560]{1,0:T(8,128)(2,1)}, s32[]{:T(128)}, pred[]{:T(512)}, /*index=5*/bf16[128,2560]...) while((s32[]{:T(128)}, bf16[64,2560]{1,0:T(8,128)(2,1)S(1)}, ...), condition=%wide.region_12.13_spmd.clone.clone, body=%wide.region_1.12_spmd.clone.clone.sunk | while | flops 6811080704 | bytes 99074000 | solution.py:112
  18.9 8.0 all-to-all-start
  26.9 47.7 %all-to-all-done = bf16[32,1,18,2560]{3,2,1,0:T(8,128)(2,1)} async-done(((bf16[32,1,18,2560]{3,2,1,0:T(8,128)(2,1)}), bf16[32,1,18,2560]{3,2,1,0:T(8,128)(2,1)}, u32[]{:S(2)}, u32[]{:S(2)}) %all-to-all-start) | async-done | bytes 2949152 | tf_op jit(solution)/shard_map/while/body/eval_jaxpr/all_to_all | solution.py:87
  78.5 7.6 all-to-all-start.1
  86.9 46.9 %all-to-all-done.1 = bf16[32,1,18,2560]{3,2,1,0:T(8,128)(2,1)} async-done(((bf16[32,1,18,2560]{3,2,1,0:T(8,128)(2,1)}), bf16[32,1,18,2560]{3,2,1,0:T(8,128)(2,1)}, u32[]{:S(2)}, u32[]{:S(2)}) %all-to-all-start.1) | async-done | bytes 2949152 | tf_op jit(solution)/shard_map/while/body/eval_jaxpr/all_to_all | solution.py:89
  147.9 8.6 collective-permute-done
  171.3 7.1 all-to-all-start
  178.4 47.7 %all-to-all-done = bf16[32,1,18,2560]{3,2,1,0:T(8,128)(2,1)} async-done(((bf16[32,1,18,2560]{3,2,1,0:T(8,128)(2,1)}), bf16[32,1,18,2560]{3,2,1,0:T(8,128)(2,1)}, u32[]{:S(2)}, u32[]{:S(2)}) %all-to-all-start) | async-done | bytes 2949152 | tf_op jit(solution)/shard_map/while/body/eval_jaxpr/all_to_all | solution.py:87
  229.9 7.6 all-to-all-start.1
  238.4 46.9 %all-to-all-done.1 = bf16[32,1,18,2560]{3,2,1,0:T(8,128)(2,1)} async-done(((bf16[32,1,18,2560]{3,2,1,0:T(8,128)(2,1)}), bf16[32,1,18,2560]{3,2,1,0:T(8,128)(2,1)}, u32[]{:S(2)}, u32[]{:S(2)}) %all-to-all-start.1) | async-done | bytes 2949152 | tf_op jit(solution)/shard_map/while/body/eval_jaxpr/all_to_all | solution.py:89
  299.3 8.6 collective-permute-done
  322.8 7.1 all-to-all-start
  329.9 47.7 %all-to-all-done = bf16[32,1,18,2560]{3,2,1,0:T(8,128)(2,1)} async-done(((bf16[32,1,18,2560]{3,2,1,0:T(8,128)(2,1)}), bf16[32,1,18,2560]{3,2,1,0:T(8,128)(2,1)}, u32[]{:S(2)}, u32[]{:S(2)}) %all-to-all-start) | async-done | bytes 2949152 | tf_op jit(solution)/shard_map/while/body/eval_jaxpr/all_to_all | solution.py:87
  381.4 7.6 all-to-all-start.1
  389.8 46.9 %all-to-all-done.1 = bf16[32,1,18,2560]{3,2,1,0:T(8,128)(2,1)} async-done(((bf16[32,1,18,2560]{3,2,1,0:T(8,128)(2,1)}), bf16[32,1,18,2560]{3,2,1,0:T(8,128)(2,1)}, u32[]{:S(2)}, u32[]{:S(2)}) %all-to-all-start.1) | async-done | bytes 2949152 | tf_op jit(solution)/shard_map/while/body/eval_jaxpr/all_to_all | solution.py:89
  450.8 8.6 collective-permute-done
  474.3 7.1 all-to-all-start
  481.4 47.7 %all-to-all-done = bf16[32,1,18,2560]{3,2,1,0:T(8,128)(2,1)} async-done(((bf16[32,1,18,2560]{3,2,1,0:T(8,128)(2,1)}), bf16[32,1,18,2560]{3,2,1,0:T(8,128)(2,1)}, u32[]{:S(2)}, u32[]{:S(2)}) %all-to-all-start) | async-done | bytes 2949152 | tf_op jit(solution)/shard_map/while/body/eval_jaxpr/all_to_all | solution.py:87
  532.9 7.6 all-to-all-start.1
  541.3 46.9 %all-to-all-done.1 = bf16[32,1,18,2560]{3,2,1,0:T(8,128)(2,1)} async-done(((bf16[32,1,18,2560]{3,2,1,0:T(8,128)(2,1)}), bf16[32,1,18,2560]{3,2,1,0:T(8,128)(2,1)}, u32[]{:S(2)}, u32[]{:S(2)}) %all-to-all-start.1) | async-done | bytes 2949152 | tf_op jit(solution)/shard_map/while/body/eval_jaxpr/all_to_all | solution.py:89
  602.3 8.6 collective-permute-done
  625.8 7.1 all-to-all-start
  632.8 47.7 %all-to-all-done = bf16[32,1,18,2560]{3,2,1,0:T(8,128)(2,1)} async-done(((bf16[32,1,18,2560]{3,2,1,0:T(8,128)(2,1)}), bf16[32,1,18,2560]{3,2,1,0:T(8,128)(2,1)}, u32[]{:S(2)}, u32[]{:S(2)}) %all-to-all-start) | async-done | bytes 2949152 | tf_op jit(solution)/shard_map/while/body/eval_jaxpr/all_to_all | solution.py:87
  684.4 7.6 all-to-all-start.1
  692.8 46.9 %all-to-all-done.1 = bf16[32,1,18,2560]{3,2,1,0:T(8,128)(2,1)} async-done(((bf16[32,1,18,2560]{3,2,1,0:T(8,128)(2,1)}), bf16[32,1,18,2560]{3,2,1,0:T(8,128)(2,1)}, u32[]{:S(2)}, u32[]{:S(2)}) %all-to-all-start.1) | async-done | bytes 2949152 | tf_op jit(solution)/shard_map/while/body/eval_jaxpr/all_to_all | solution.py:89
  753.8 9.1 collective-permute-done
  784.6 47.7 %all-to-all-done = bf16[32,1,18,2560]{3,2,1,0:T(8,128)(2,1)} async-done(((bf16[32,1,18,2560]{3,2,1,0:T(8,128)(2,1)}), bf16[32,1,18,2560]{3,2,1,0:T(8,128)(2,1)}, u32[]{:S(2)}, u32[]{:S(2)}) %all-to-all-start) | async-done | bytes 2949152 | tf_op jit(solution)/shard_map/while/body/eval_jaxpr/all_to_all | solution.py:87
  836.2 7.6 all-to-all-start.1
  844.6 46.9 %all-to-all-done.1 = bf16[32,1,18,2560]{3,2,1,0:T(8,128)(2,1)} async-done(((bf16[32,1,18,2560]{3,2,1,0:T(8,128)(2,1)}), bf16[32,1,18,2560]{3,2,1,0:T(8,128)(2,1)}, u32[]{:S(2)}, u32[]{:S(2)}) %all-to-all-start.1) | async-done | bytes 2949152 | tf_op jit(solution)/shard_map/while/body/eval_jaxpr/all_to_all | solution.py:89
  905.6 10.1 collective-permute-done
  937.3 47.7 %all-to-all-done = bf16[32,1,18,2560]{3,2,1,0:T(8,128)(2,1)} async-done(((bf16[32,1,18,2560]{3,2,1,0:T(8,128)(2,1)}), bf16[32,1,18,2560]{3,2,1,0:T(8,128)(2,1)}, u32[]{:S(2)}, u32[]{:S(2)}) %all-to-all-start) | async-done | bytes 2949152 | tf_op jit(solution)/shard_map/while/body/eval_jaxpr/all_to_all | solution.py:87
  988.9 7.6 all-to-all-start.1
  997.3 46.9 %all-to-all-done.1 = bf16[32,1,18,2560]{3,2,1,0:T(8,128)(2,1)} async-done(((bf16[32,1,18,2560]{3,2,1,0:T(8,128)(2,1)}), bf16[32,1,18,2560]{3,2,1,0:T(8,128)(2,1)}, u32[]{:S(2)}, u32[]{:S(2)}) %all-to-all-start.1) | async-done | bytes 2949152 | tf_op jit(solution)/shard_map/while/body/eval_jaxpr/all_to_all | solution.py:89
  1058.3 125.7 %collective-permute-done = bf16[64,2560]{1,0:T(8,128)(2,1)S(1)} collective-permute-done((bf16[64,2560]{1,0:T(8,128)(2,1)S(1)}, bf16[64,2560]{1,0:T(8,128)(2,1)S(1)}, u32[]{:S(2)}, u32[]{:S(2)}) %collective-permute-start) | collective-permute-done | bytes 327712 | tf_op jit(solution)/shard_map/while/body/eval_jaxpr/ppermute | solution.py:12
  1205.6 47.7 %all-to-all-done = bf16[32,1,18,2560]{3,2,1,0:T(8,128)(2,1)} async-done(((bf16[32,1,18,2560]{3,2,1,0:T(8,128)(2,1)}), bf16[32,1,18,2560]{3,2,1,0:T(8,128)(2,1)}, u32[]{:S(2)}, u32[]{:S(2)}) %all-to-all-start) | async-done | bytes 2949152 | tf_op jit(solution)/shard_map/while/body/eval_jaxpr/all_to_all | solution.py:87
  1253.3 18.5 %conditional.4 = (bf16[32,1,18,2560]{3,0,2,1:T(8,128)(2,1)S(1)}) conditional(s32[]{:T(128)} %convert_element_type.144, () %tuple.70, (bf16[1,2560,768]{2,1,0:T(8,128)(2,1)}, bf16[32,1,18,2560]{3,2,1,0:T(8,128)(2,1)}, bf16[1,2560,768]{2,1,0:T(8,128)(2,1)}, bf16[1,768,2560]{2,1,0:T(8,128)(2,1)}) %tuple.71), branch_computations={%region_9.9_spmd, %region_10.10_spmd} | conditional | flops 6798901248 | bytes 24182792 | solution.py:83
  1253.3 7.1 fusion.4
  1260.5 11.4 fusion.2
  1275.4 7.6 all-to-all-start.1
  1283.8 46.9 %all-to-all-done.1 = bf16[32,1,18,2560]{3,2,1,0:T(8,128)(2,1)} async-done(((bf16[32,1,18,2560]{3,2,1,0:T(8,128)(2,1)}), bf16[32,1,18,2560]{3,2,1,0:T(8,128)(2,1)}, u32[]{:S(2)}, u32[]{:S(2)}) %all-to-all-start.1) | async-done | bytes 2949152 | tf_op jit(solution)/shard_map/while/body/eval_jaxpr/all_to_all | solution.py:89
  1344.8 10.1 collective-permute-done
  1376.5 47.7 %all-to-all-done = bf16[32,1,18,2560]{3,2,1,0:T(8,128)(2,1)} async-done(((bf16[32,1,18,2560]{3,2,1,0:T(8,128)(2,1)}), bf16[32,1,18,2560]{3,2,1,0:T(8,128)(2,1)}, u32[]{:S(2)}, u32[]{:S(2)}) %all-to-all-start) | async-done | bytes 2949152 | tf_op jit(solution)/shard_map/while/body/eval_jaxpr/all_to_all | solution.py:87
  1424.3 18.5 %conditional.4 = (bf16[32,1,18,2560]{3,0,2,1:T(8,128)(2,1)S(1)}) conditional(s32[]{:T(128)} %convert_element_type.144, () %tuple.70, (bf16[1,2560,768]{2,1,0:T(8,128)(2,1)}, bf16[32,1,18,2560]{3,2,1,0:T(8,128)(2,1)}, bf16[1,2560,768]{2,1,0:T(8,128)(2,1)}, bf16[1,768,2560]{2,1,0:T(8,128)(2,1)}) %tuple.71), branch_computations={%region_9.9_spmd, %region_10.10_spmd} | conditional | flops 6798901248 | bytes 24182792 | solution.py:83
  1424.3 7.1 fusion.4
  1431.4 11.4 fusion.2
  1446.3 7.6 all-to-all-start.1
  1454.7 46.9 %all-to-all-done.1 = bf16[32,1,18,2560]{3,2,1,0:T(8,128)(2,1)} async-done(((bf16[32,1,18,2560]{3,2,1,0:T(8,128)(2,1)}), bf16[32,1,18,2560]{3,2,1,0:T(8,128)(2,1)}, u32[]{:S(2)}, u32[]{:S(2)}) %all-to-all-start.1) | async-done | bytes 2949152 | tf_op jit(solution)/shard_map/while/body/eval_jaxpr/all_to_all | solution.py:89
  1515.7 8.6 collective-permute-done
  (519 shorter events, 332.3 us)
Async XLA Ops:
  18.9 55.7 %all-to-all-start = ((bf16[32,1,18,2560]{3,2,1,0:T(8,128)(2,1)}), bf16[32,1,18,2560]{3,2,1,0:T(8,128)(2,1)}, u32[]{:S(2)}, u32[]{:S(2)}) async-start(bf16[32,1,18,2560]{3,2,1,0:T(8,128)(2,1)} %select_bitcast_fusion.2), calls=%async_computation | async-start | bytes 7864320 | tf_op jit(solution)/shard_map/while/body/eval_jaxpr/all_to_all | solution.py:87
  78.5 55.3 %all-to-all-start.1 = ((bf16[32,1,18,2560]{3,2,1,0:T(8,128)(2,1)}), bf16[32,1,18,2560]{3,2,1,0:T(8,128)(2,1)}, u32[]{:S(2)}, u32[]{:S(2)}) async-start(bf16[32,1,18,2560]{3,2,1,0:T(8,128)(2,1)} %copy.68), calls=%async_computation.1 | async-start | bytes 7864320 | tf_op jit(solution)/shard_map/while/body/eval_jaxpr/all_to_all | solution.py:89
  140.4 5.2 copy-start.1
  143.0 2.5 copy-start.2
  145.7 0.8 copy-start.3
  146.6 9.9 collective-permute-start
  171.3 54.8 %all-to-all-start = ((bf16[32,1,18,2560]{3,2,1,0:T(8,128)(2,1)}), bf16[32,1,18,2560]{3,2,1,0:T(8,128)(2,1)}, u32[]{:S(2)}, u32[]{:S(2)}) async-start(bf16[32,1,18,2560]{3,2,1,0:T(8,128)(2,1)} %select_bitcast_fusion.2), calls=%async_computation | async-start | bytes 7864320 | tf_op jit(solution)/shard_map/while/body/eval_jaxpr/all_to_all | solution.py:87
  229.9 55.3 %all-to-all-start.1 = ((bf16[32,1,18,2560]{3,2,1,0:T(8,128)(2,1)}), bf16[32,1,18,2560]{3,2,1,0:T(8,128)(2,1)}, u32[]{:S(2)}, u32[]{:S(2)}) async-start(bf16[32,1,18,2560]{3,2,1,0:T(8,128)(2,1)} %copy.68), calls=%async_computation.1 | async-start | bytes 7864320 | tf_op jit(solution)/shard_map/while/body/eval_jaxpr/all_to_all | solution.py:89
  291.8 5.2 copy-start.1
  294.5 2.5 copy-start.2
  298.1 9.9 collective-permute-start
  322.8 54.8 %all-to-all-start = ((bf16[32,1,18,2560]{3,2,1,0:T(8,128)(2,1)}), bf16[32,1,18,2560]{3,2,1,0:T(8,128)(2,1)}, u32[]{:S(2)}, u32[]{:S(2)}) async-start(bf16[32,1,18,2560]{3,2,1,0:T(8,128)(2,1)} %select_bitcast_fusion.2), calls=%async_computation | async-start | bytes 7864320 | tf_op jit(solution)/shard_map/while/body/eval_jaxpr/all_to_all | solution.py:87
  381.4 55.3 %all-to-all-start.1 = ((bf16[32,1,18,2560]{3,2,1,0:T(8,128)(2,1)}), bf16[32,1,18,2560]{3,2,1,0:T(8,128)(2,1)}, u32[]{:S(2)}, u32[]{:S(2)}) async-start(bf16[32,1,18,2560]{3,2,1,0:T(8,128)(2,1)} %copy.68), calls=%async_computation.1 | async-start | bytes 7864320 | tf_op jit(solution)/shard_map/while/body/eval_jaxpr/all_to_all | solution.py:89
  443.3 5.2 copy-start.1
  446.0 2.5 copy-start.2
  449.5 9.9 collective-permute-start
  474.3 54.8 %all-to-all-start = ((bf16[32,1,18,2560]{3,2,1,0:T(8,128)(2,1)}), bf16[32,1,18,2560]{3,2,1,0:T(8,128)(2,1)}, u32[]{:S(2)}, u32[]{:S(2)}) async-start(bf16[32,1,18,2560]{3,2,1,0:T(8,128)(2,1)} %select_bitcast_fusion.2), calls=%async_computation | async-start | bytes 7864320 | tf_op jit(solution)/shard_map/while/body/eval_jaxpr/all_to_all | solution.py:87
  532.9 55.3 %all-to-all-start.1 = ((bf16[32,1,18,2560]{3,2,1,0:T(8,128)(2,1)}), bf16[32,1,18,2560]{3,2,1,0:T(8,128)(2,1)}, u32[]{:S(2)}, u32[]{:S(2)}) async-start(bf16[32,1,18,2560]{3,2,1,0:T(8,128)(2,1)} %copy.68), calls=%async_computation.1 | async-start | bytes 7864320 | tf_op jit(solution)/shard_map/while/body/eval_jaxpr/all_to_all | solution.py:89
  594.8 5.2 copy-start.1
  597.5 2.5 copy-start.2
  600.2 0.8 copy-start.3
  601.0 9.9 collective-permute-start
  625.8 54.8 %all-to-all-start = ((bf16[32,1,18,2560]{3,2,1,0:T(8,128)(2,1)}), bf16[32,1,18,2560]{3,2,1,0:T(8,128)(2,1)}, u32[]{:S(2)}, u32[]{:S(2)}) async-start(bf16[32,1,18,2560]{3,2,1,0:T(8,128)(2,1)} %select_bitcast_fusion.2), calls=%async_computation | async-start | bytes 7864320 | tf_op jit(solution)/shard_map/while/body/eval_jaxpr/all_to_all | solution.py:87
  684.4 55.3 %all-to-all-start.1 = ((bf16[32,1,18,2560]{3,2,1,0:T(8,128)(2,1)}), bf16[32,1,18,2560]{3,2,1,0:T(8,128)(2,1)}, u32[]{:S(2)}, u32[]{:S(2)}) async-start(bf16[32,1,18,2560]{3,2,1,0:T(8,128)(2,1)} %copy.68), calls=%async_computation.1 | async-start | bytes 7864320 | tf_op jit(solution)/shard_map/while/body/eval_jaxpr/all_to_all | solution.py:89
  746.3 5.2 copy-start.1
  749.0 2.5 copy-start.2
  752.5 10.4 collective-permute-start
  777.8 54.5 %all-to-all-start = ((bf16[32,1,18,2560]{3,2,1,0:T(8,128)(2,1)}), bf16[32,1,18,2560]{3,2,1,0:T(8,128)(2,1)}, u32[]{:S(2)}, u32[]{:S(2)}) async-start(bf16[32,1,18,2560]{3,2,1,0:T(8,128)(2,1)} %select_bitcast_fusion.2), calls=%async_computation | async-start | bytes 7864320 | tf_op jit(solution)/shard_map/while/body/eval_jaxpr/all_to_all | solution.py:87
  836.2 55.3 %all-to-all-start.1 = ((bf16[32,1,18,2560]{3,2,1,0:T(8,128)(2,1)}), bf16[32,1,18,2560]{3,2,1,0:T(8,128)(2,1)}, u32[]{:S(2)}, u32[]{:S(2)}) async-start(bf16[32,1,18,2560]{3,2,1,0:T(8,128)(2,1)} %copy.68), calls=%async_computation.1 | async-start | bytes 7864320 | tf_op jit(solution)/shard_map/while/body/eval_jaxpr/all_to_all | solution.py:89
  898.1 5.2 copy-start.1
  900.7 2.5 copy-start.2
  904.3 11.4 collective-permute-start
  930.5 54.5 %all-to-all-start = ((bf16[32,1,18,2560]{3,2,1,0:T(8,128)(2,1)}), bf16[32,1,18,2560]{3,2,1,0:T(8,128)(2,1)}, u32[]{:S(2)}, u32[]{:S(2)}) async-start(bf16[32,1,18,2560]{3,2,1,0:T(8,128)(2,1)} %select_bitcast_fusion.2), calls=%async_computation | async-start | bytes 7864320 | tf_op jit(solution)/shard_map/while/body/eval_jaxpr/all_to_all | solution.py:87
  988.9 55.3 %all-to-all-start.1 = ((bf16[32,1,18,2560]{3,2,1,0:T(8,128)(2,1)}), bf16[32,1,18,2560]{3,2,1,0:T(8,128)(2,1)}, u32[]{:S(2)}, u32[]{:S(2)}) async-start(bf16[32,1,18,2560]{3,2,1,0:T(8,128)(2,1)} %copy.68), calls=%async_computation.1 | async-start | bytes 7864320 | tf_op jit(solution)/shard_map/while/body/eval_jaxpr/all_to_all | solution.py:89
  1050.8 5.2 copy-start.1
  1053.4 2.5 copy-start.2
  1057.0 127.0 %collective-permute-start = (bf16[64,2560]{1,0:T(8,128)(2,1)S(1)}, bf16[64,2560]{1,0:T(8,128)(2,1)S(1)}, u32[]{:S(2)}, u32[]{:S(2)}) collective-permute-start(bf16[64,2560]{1,0:T(8,128)(2,1)S(1)} %get-tuple-element.549), channel_id=1, source_target_pairs={{0,32},{32,64},{64,96},{96,128},{128,160},{160,192},{192,224},{1,3... | collective-permute-start | bytes 983048 | tf_op jit(solution)/shard_map/while/body/eval_jaxpr/ppermute | solution.py:12
  1198.8 54.5 %all-to-all-start = ((bf16[32,1,18,2560]{3,2,1,0:T(8,128)(2,1)}), bf16[32,1,18,2560]{3,2,1,0:T(8,128)(2,1)}, u32[]{:S(2)}, u32[]{:S(2)}) async-start(bf16[32,1,18,2560]{3,2,1,0:T(8,128)(2,1)} %select_bitcast_fusion.2), calls=%async_computation | async-start | bytes 7864320 | tf_op jit(solution)/shard_map/while/body/eval_jaxpr/all_to_all | solution.py:87
  1275.4 55.4 %all-to-all-start.1 = ((bf16[32,1,18,2560]{3,2,1,0:T(8,128)(2,1)}), bf16[32,1,18,2560]{3,2,1,0:T(8,128)(2,1)}, u32[]{:S(2)}, u32[]{:S(2)}) async-start(bf16[32,1,18,2560]{3,2,1,0:T(8,128)(2,1)} %copy.68), calls=%async_computation.1 | async-start | bytes 7864320 | tf_op jit(solution)/shard_map/while/body/eval_jaxpr/all_to_all | solution.py:89
  1337.3 5.2 copy-start.1
  1340.0 2.5 copy-start.2
  1342.7 0.8 copy-start.3
  1343.5 11.4 collective-permute-start
  1369.8 54.5 %all-to-all-start = ((bf16[32,1,18,2560]{3,2,1,0:T(8,128)(2,1)}), bf16[32,1,18,2560]{3,2,1,0:T(8,128)(2,1)}, u32[]{:S(2)}, u32[]{:S(2)}) async-start(bf16[32,1,18,2560]{3,2,1,0:T(8,128)(2,1)} %select_bitcast_fusion.2), calls=%async_computation | async-start | bytes 7864320 | tf_op jit(solution)/shard_map/while/body/eval_jaxpr/all_to_all | solution.py:87
  1446.3 55.4 %all-to-all-start.1 = ((bf16[32,1,18,2560]{3,2,1,0:T(8,128)(2,1)}), bf16[32,1,18,2560]{3,2,1,0:T(8,128)(2,1)}, u32[]{:S(2)}, u32[]{:S(2)}) async-start(bf16[32,1,18,2560]{3,2,1,0:T(8,128)(2,1)} %copy.68), calls=%async_computation.1 | async-start | bytes 7864320 | tf_op jit(solution)/shard_map/while/body/eval_jaxpr/all_to_all | solution.py:89
  1508.2 5.2 copy-start.1
  1510.9 2.5 copy-start.2
  1514.4 9.9 collective-permute-start
  (15 other events, 11.7 us)
where the time goes:
time: 1530 us; the launch traced here: 1520 us
  waiting for transfers between devices  1050 us (69%)
  local copies, waits for them, and re-layouts  202 us (13%)
  starting transfers between devices  143 us (9%)
  other arithmetic  89.1 us (6%)
  matrix products  37 us (2%)
    all_to_all x9, waiting for transfers between devices, run_piece(): lax.all_to_all(outgoing, 'expert', split_axis=0, concat_axis=0, tiled=True)  430 us
    all_to_all x9, waiting for transfers between devices, run_piece(): lax.all_to_all(computed, 'expert', split_axis=0, concat_axis=0, tiled=True)  422 us
    ppermute x9, waiting for transfers between devices, passed_along(): lax.ppermute(value, axis, [(source, source + steps) for source in range(l...  198 us
    all_to_all x9, starting transfers between devices, run_piece(): lax.all_to_all(computed, 'expert', split_axis=0, concat_axis=0, tiled=True)  68.4 us
    all_to_all x9, starting transfers between devices, run_piece(): lax.all_to_all(outgoing, 'expert', split_axis=0, concat_axis=0, tiled=True)  63.2 us
    gather x18, local copies, waits for them, and re-layouts, run_piece(): jnp.take(normed, source, axis=0)  57.1 us
    gather x18, local copies, waits for them, and re-layouts, run_piece(): jnp.take(answers.reshape(slot_count * capacity, model_width), target, axi...  53.7 us
    select_n x9, other arithmetic, run_piece(): jnp.where(filled[:, None], jnp.take(normed, source, axis=0), jnp.zeros(()...  33.9 us
  transfers between devices with their start and end apart: 27, of which 27 were waited for; matrix products, arithmetic and copies ran while one was open for 0% of the time, Pallas kernels for 0%

commit v1 on v0

v1 whole, which is shorter than its diff:
```python
import functools

import jax
import jax.numpy as jnp
from jax import lax
from jax.experimental import pallas as pl
from jax.experimental.pallas import tpu as pltpu
from jax.sharding import PartitionSpec as P

MESH = pl.DeviceIdType.MESH
epsilon = 1e-06
SIDE = 4
ROWS = 16


def layer_kernel(
    planes, pieces,
    act, gain, weight_table, gate_hbm, up_hbm, down_hbm,
    out,
    wg, wu, wd, xg, xn, hidden, rs1, rs2, rs3, part_o, part_m, fbuf, obuf,
    w_sem, x_recv, y_send, y_recv, s_send, s_recv, d_send, r1_recv, e_send, r2_recv, f_send, r3_recv,
    g_send, o_send, o_recv, i_send,
):
    half = xg.shape[-1]
    ff = wg.shape[-1]
    total = SIDE * SIDE * ROWS
    z = lax.axis_index("pipe")
    e = lax.axis_index("expert")
    core = e % 2
    chip = e // 2
    x, y = chip % SIDE, chip // SIDE
    other = 1 - core
    u = x * other + y * core
    v = y * other + x * core
    su, sv = 2 + (2 * SIDE - 2) * core, 2 * SIDE - (2 * SIDE - 2) * core

    def dev(u_at, v_at):
        return u_at * su + v_at * sv + core

    sibling = u * su + v * sv + other

    def cross(u_at, v_at):
        return u_at * su + v_at * sv + other

    def wait(sem, ref):
        pltpu.make_async_copy(ref, ref, sem).wait()

    def send(src, dst, send_sem, recv_sem, plane, device):
        pltpu.make_async_remote_copy(
            src_ref=src, dst_ref=dst, send_sem=send_sem, recv_sem=recv_sem,
            device_id=(plane, device), device_id_type=MESH,
        ).start()

    loads = []
    own = pl.ds(pl.multiple_of(core * half, 128), half)
    oth = pl.ds(pl.multiple_of(other * half, 128), half)
    for at, part in ((0, own), (1, oth)):
        rows = pl.ds(at * half, half)
        loads.append(pltpu.make_async_copy(gate_hbm.at[0, 0, part], wg.at[rows], w_sem.at[at]))
        loads.append(pltpu.make_async_copy(up_hbm.at[0, 0, part], wu.at[rows], w_sem.at[2 + at]))
        loads.append(
            pltpu.make_async_copy(down_hbm.at[0, 0, :, part], wd.at[at], w_sem.at[4 + at])
        )
    for load in loads:
        load.start()

    barrier = pltpu.get_barrier_semaphore()

    def greet(plane, device):
        pl.semaphore_signal(barrier, inc=1, device_id=(plane, device), device_id_type=MESH)

    greet(z, sibling)
    for k in range(1, SIDE):
        greet(z, dev(lax.rem(u + k, SIDE), v))
        greet(z, dev(u, lax.rem(v + k, SIDE)))

    @pl.when(z > 0)
    def _():
        for k in range(SIDE):
            greet(z - 1, dev(k, v))

    @pl.when(z == 0)
    def _():
        for k in range(1, SIDE):
            greet(z, cross(lax.rem(u + k, SIDE), v))

    first, last = jnp.where(z == 0, 1, 0), jnp.where(z == planes - 1, 1, 0)
    pl.semaphore_wait(barrier, 2 * SIDE - 1 + (SIDE - 1) * first + SIDE * (1 - last))

    def inject(p):
        q = p // 2

        @pl.when((z == 0) & (p < pieces) & (p % 2 == core))
        def _():
            pltpu.make_async_copy(act.at[core, q], xg.at[p, 0, v, u], x_recv.at[p]).start()
            for k in range(1, SIDE):
                send(act.at[core, q], xg.at[p, 0, v, u], i_send.at[p, 0], x_recv.at[p],
                     z, dev(lax.rem(u + k, SIDE), v))
            for k in range(SIDE):
                send(act.at[other, q], xg.at[p, 0, u, v], i_send.at[p, 1], x_recv.at[p],
                     z, cross(u, lax.rem(v + k, SIDE)))

    def relay(p, at):
        send(xg.at[p, 0, at], xg.at[p, 1, :, at], s_send.at[p], s_recv.at[p], z, sibling)

    def stage_a(p):
        wait(x_recv.at[p], xg.at[p, 0, v])
        for k in (2, 1, 3):
            send(xg.at[p, 0, v], xg.at[p, 0, v], y_send.at[p, k - 1], y_recv.at[p, k - 1],
                 z, dev(u, lax.rem(v + k, SIDE)))
        relay(p, v)

    def stage_b(p):
        for k in (1, 3, 2):
            at = lax.rem(v + SIDE - k, SIDE)
            wait(y_recv.at[p, k - 1], xg.at[p, 0, at])
            relay(p, at)

    def stage_norm(p):
        wait(s_recv.at[p], xg.at[p, 1])

        def block(r, _):
            for c in range(SIDE):
                x0 = xg[p, 0, r, c].astype(jnp.float32)
                x1 = xg[p, 1, r, c].astype(jnp.float32)
                square = jnp.sum(x0 * x0, axis=-1, keepdims=True)
                square = square + jnp.sum(x1 * x1, axis=-1, keepdims=True)
                inverse = lax.rsqrt(square / (2 * half) + epsilon)
                xn[r, c, :, 0:half] = (x0 * inverse * gain[0]).astype(jnp.bfloat16)
                xn[r, c, :, half:] = (x1 * inverse * gain[1]).astype(jnp.bfloat16)
            return 0

        lax.fori_loop(0, SIDE, block, 0)

    def stage_up(p):
        lane = lax.broadcasted_iota(jnp.int32, weight_table.shape, 1)
        scale = jnp.sum(jnp.where(lane == p, weight_table[...], 0.0), axis=1, keepdims=True)
        step = min(256, ff)
        rows = xn[...].reshape(total, 2 * half)
        for n in range(0, ff, step):
            gate_value = jnp.dot(rows, wg[:, n : n + step], preferred_element_type=jnp.float32)
            up_value = jnp.dot(rows, wu[:, n : n + step], preferred_element_type=jnp.float32)
            value = gate_value / (1.0 + jnp.exp(-gate_value)) * up_value * scale
            hidden[:, n : n + step] = value.astype(jnp.bfloat16)

    def stage_down(p):
        slot = p % 2

        @pl.when(p >= 2)
        def _():
            wait(d_send.at[p - 2], part_o.at[slot])
            wait(e_send.at[p - 2], part_m.at[slot, 0 : SIDE - 1])

        step = min(256, half)
        for at, part in ((1, part_o), (0, part_m)):
            for n in range(0, half, step):
                value = jnp.dot(
                    hidden[...], wd[at, :, n : n + step], preferred_element_type=jnp.float32
                )
                part[slot, :, :, :, n : n + step] = value.astype(jnp.bfloat16).reshape(
                    SIDE, SIDE, ROWS, step
                )
            if at == 1:
                for k in range(SIDE):
                    send(part_o.at[slot, k], rs1.at[slot, :, k], d_send.at[p], r1_recv.at[p],
                         z, sibling)

    def stage_e(p):
        slot = p % 2
        wait(r1_recv.at[p], rs1.at[slot])
        for k in (2, 1, 3, 0):
            at = lax.rem(v + k, SIDE)
            value = part_m[slot, at].astype(jnp.float32) + rs1[slot, at].astype(jnp.float32)
            part_m[slot, at] = value.astype(jnp.bfloat16)
            if k:
                send(part_m.at[slot, at], rs2.at[slot, k - 1], e_send.at[p], r2_recv.at[p],
                     z, dev(u, at))

    def stage_f(p):
        slot = p % 2
        wait(r2_recv.at[p], rs2.at[slot])

        @pl.when(p >= 2)
        def _():
            wait(f_send.at[p - 2], fbuf.at[slot, 0 : SIDE - 1])

        for k in (2, 1, 3, 0):
            at = lax.rem(u + k, SIDE)
            value = part_m[slot, v, at].astype(jnp.float32)
            for j in range(SIDE - 1):
                value = value + rs2[slot, j, at].astype(jnp.float32)
            fbuf[slot, at] = value.astype(jnp.bfloat16)
            if k:
                send(fbuf.at[slot, at], rs3.at[p, k - 1], f_send.at[p], r3_recv.at[p],
                     z, dev(at, v))

    def stage_g(p):
        slot = p % 2
        q = p // 2
        wait(r3_recv.at[p], rs3.at[p])
        value = xg[p, 0, v, u].astype(jnp.float32) + fbuf[slot, u].astype(jnp.float32)
        for j in range(SIDE - 1):
            value = value + rs3[p, j].astype(jnp.float32)
        obuf[p] = value.astype(jnp.bfloat16)

        @pl.when(z < planes - 1)
        def _():
            for k in range(SIDE):
                send(obuf.at[p], xg.at[p, 0, v, u], g_send.at[p], x_recv.at[p],
                     z + 1, dev(lax.rem(u + k, SIDE), v))

        @pl.when(p % 2 == core)
        def _():
            pltpu.make_async_copy(obuf.at[p], out.at[core, q], o_send.at[p]).start()

        @pl.when(p % 2 == other)
        def _():
            send(obuf.at[p], out.at[core, q], o_send.at[p], o_recv.at[p], z, sibling)

    inject(0)
    inject(1)

    def iteration(i, _):
        @pl.when(i < pieces)
        def _():
            stage_a(i)
            inject(i + 2)

        @pl.when(i >= 1)
        def _():
            stage_e(i - 1)

        @pl.when(i == 0)
        def _():
            for load in loads:
                load.wait()

        @pl.when(i < pieces)
        def _():
            stage_b(i)
            stage_norm(i)
            stage_up(i)

        @pl.when(i >= 1)
        def _():
            stage_f(i - 1)

        @pl.when(i < pieces)
        def _():
            stage_down(i)

        @pl.when(i >= 1)
        def _():
            stage_g(i - 1)

        return 0

    lax.fori_loop(0, pieces + 1, iteration, 0)

    def drain(p, _):
        for k in range(1, SIDE):
            wait(y_send.at[p, k - 1], xg.at[p, 0, v])
        wait(s_send.at[p], xg.at[p, 0])

        @pl.when(p >= pieces - 2)
        def _():
            wait(d_send.at[p], part_o.at[0])
            wait(e_send.at[p], part_m.at[0, 0 : SIDE - 1])
            wait(f_send.at[p], fbuf.at[0, 0 : SIDE - 1])

        @pl.when(z < planes - 1)
        def _():
            wait(g_send.at[p], xg.at[p, 0, v])

        wait(o_send.at[p], obuf.at[p])

        @pl.when(p % 2 == core)
        def _():
            wait(o_recv.at[p], obuf.at[p])

        @pl.when((z == 0) & (p % 2 == core))
        def _():
            wait(i_send.at[p, 0], xg.at[p, 0, v, 0 : SIDE - 1])
            wait(i_send.at[p, 1], xg.at[p, 0, v])

        return 0

    lax.fori_loop(0, pieces, drain, 0)


def on_device(
    activations, norm_gain, placement, expert_ids, expert_weights, gate_store, up_store, down_store
):
    planes = lax.axis_size("pipe")
    group = lax.axis_size("expert")
    core = lax.axis_index("expert") % 2
    micro, rows_local, width = activations.shape
    half = width // 2
    ff = gate_store.shape[-1]
    rows = micro * rows_local
    depth = rows // ROWS
    pieces = 2 * depth
    total = SIDE * SIDE * ROWS
    bf16 = jnp.bfloat16

    ids = expert_ids.reshape(1, rows, -1)
    weights = expert_weights.reshape(1, rows, -1)
    named = jnp.where(ids == placement[0][:, None, None], weights, 0.0)
    dense = jnp.sum(named, axis=-1)
    mine = lax.all_to_all(dense, "expert", split_axis=0, concat_axis=0, tiled=True)
    mine = mine.reshape(SIDE, SIDE, 2, depth, ROWS)
    table = jnp.where(
        core == 0, mine.transpose(0, 1, 4, 3, 2), mine.transpose(1, 0, 4, 3, 2)
    ).reshape(total, pieces)

    act = activations.reshape(depth, ROWS, 2, half).transpose(2, 0, 1, 3)
    gain = norm_gain[0].astype(jnp.float32).reshape(2, 1, half)
    gain = jnp.where(core == 0, gain, gain[::-1])

    dma = pltpu.SemaphoreType.DMA
    vmem = pl.BlockSpec(memory_space=pltpu.VMEM)
    hbm = pl.BlockSpec(memory_space=pl.ANY)
    out = pl.pallas_call(
        functools.partial(layer_kernel, planes, pieces),
        out_shape=jax.ShapeDtypeStruct((2, depth, ROWS, half), bf16),
        in_specs=[vmem, vmem, vmem, hbm, hbm, hbm],
        out_specs=vmem,
        scratch_shapes=[
            pltpu.VMEM((width, ff), bf16),
            pltpu.VMEM((width, ff), bf16),
            pltpu.VMEM((2, ff, half), bf16),
            pltpu.VMEM((pieces, 2, SIDE, SIDE, ROWS, half), bf16),
            pltpu.VMEM((SIDE, SIDE, ROWS, width), bf16),
            pltpu.VMEM((total, ff), bf16),
            pltpu.VMEM((2, SIDE, SIDE, ROWS, half), bf16),
            pltpu.VMEM((2, SIDE - 1, SIDE, ROWS, half), bf16),
            pltpu.VMEM((pieces, SIDE - 1, ROWS, half), bf16),
            pltpu.VMEM((2, SIDE, SIDE, ROWS, half), bf16),
            pltpu.VMEM((2, SIDE, SIDE, ROWS, half), bf16),
            pltpu.VMEM((2, SIDE, ROWS, half), bf16),
            pltpu.VMEM((pieces, ROWS, half), bf16),
            dma((6,)),
            dma((pieces,)),
            dma((pieces, SIDE - 1)),
            dma((pieces, SIDE - 1)),
            dma((pieces,)),
            dma((pieces,)),
            dma((pieces,)),
            dma((pieces,)),
            dma((pieces,)),
            dma((pieces,)),
            dma((pieces,)),
            dma((pieces,)),
            dma((pieces,)),
            dma((pieces,)),
            dma((pieces,)),
            dma((pieces, 2)),
        ],
        compiler_params=pltpu.CompilerParams(
            collective_id=0, has_side_effects=True, vmem_limit_bytes=60 * 2**20
        ),
        name="layers",
    )(act, gain, table, gate_store, up_store, down_store)
    return out.transpose(1, 2, 0, 3).reshape(1, micro, rows_local, width)


def solution(mesh):
    in_specs = (
        P(None, "expert", None),
        P("pipe", None),
        P("pipe", None),
        P("pipe", None, "expert", None),
        P("pipe", None, "expert", None),
        P("pipe", "expert", None, None),
        P("pipe", "expert", None, None),
        P("pipe", "expert", None, None),
    )
    out_specs = P("pipe", None, "expert", None)
    return jax.shard_map(
        on_device, mesh=mesh, in_specs=in_specs, out_specs=out_specs, check_vma=False
    )
```

time: 1530 us -> 536 us (0.35)
  waiting for transfers between devices: 1050 us -> 1.56 us
  Pallas kernels: 0 us -> 512 us
  local copies, waits for them, and re-layouts: 202 us -> 9.17 us
  starting transfers between devices: 143 us -> 7.93 us
  other arithmetic: 89.1 us -> 3.38 us
  matrix products: 37 us -> 0 us
    all_to_all x18 -> x1, waiting for transfers between devices: 852 us -> 1.56 us  [on_device(): lax.all_to_all(dense, 'expert', split_axis=0, concat_axis=0, tiled=True)]
    pallas_call x0 -> x1, Pallas kernels: none -> 512 us  [on_device(): pl.pallas_call(functools.partial(layer_kernel, planes, pieces), out_shape...]
    ppermute x9 -> x0, waiting for transfers between devices: 198 us -> none  [passed_along(): lax.ppermute(value, axis, [(source, source + steps) for source in range(l...]
    all_to_all x18 -> x1, starting transfers between devices: 132 us -> 7.93 us  [on_device(): lax.all_to_all(dense, 'expert', split_axis=0, concat_axis=0, tiled=True)]
    gather x36 -> x0, local copies, waits for them, and re-layouts: 111 us -> none  [the longest x18 57.1 us: run_piece(): jnp.take(normed, source, axis=0)]
    dot_general x4 -> x0, matrix products: 37 us -> none  [the longest x2 22.8 us: expert_compute(): jnp.einsum('sjrf,jfd->sjrd', hidden, down_w, preferred_element_type=jnp.f...]
    reduce_sum x37 -> x1, other arithmetic: 36.6 us -> 1.33 us  [on_device(): dense = jnp.sum(named, axis=-1)]
    select_n x36 -> x2, other arithmetic: 34.3 us -> 0.61 us  [the longest x1 0.6 us: on_device(): gain = jnp.where(core == 0, gain, gain[::-1])]
  transfers between devices with their start and end apart: 27 -> 1, of which waited for: 27 -> 1; matrix products, arithmetic and copies ran while one was open for 0% -> 1% of each run, Pallas kernels for 0% -> 0%
where the time goes in v1:
time: 536 us; the launch traced here: 534 us
  Pallas kernels  512 us (96%)
  local copies, waits for them, and re-layouts  9.17 us (2%)
  starting transfers between devices  7.93 us (1%)
    pallas_call x1, Pallas kernels, on_device(): pl.pallas_call(functools.partial(layer_kernel, planes, pieces), out_shape...  512 us
  transfers between devices with their start and end apart: 1, of which 1 were waited for; matrix products, arithmetic and copies ran while one was open for 1% of the time, Pallas kernels for 0%

profile of v1, /device:TPU:227, one launch (start us, length us, event | category | flops | bytes accessed | tf_op | source)
XLA Modules:
  0.0 534.3 jit_solution(11382553119808079601)
XLA Ops:
  0.0 0.8 eq.24
  0.8 0.8 broadcast_in_dim.14
  1.5 1.3 select_reduce_fusion
  2.9 7.9 %all-to-all-start = ((f32[32,1,128]{2,1,0:T(1,128)}), f32[32,1,128]{2,1,0:T(1,128)S(1)}, u32[]{:S(2)}, u32[]{:S(2)}) async-start(f32[32,1,128]{2,1,0:T(1,128)} %bitcast.5), calls=%async_computation | async-start | bytes 32768 | tf_op jit(solution)/shard_map/all_to_all | solution.py:310
  10.8 0.7 convert.1
  11.5 0.6 broadcast_select_fusion.gain
  12.1 2.1 reshape.33
  14.2 0.9 copy.34
  15.1 1.6 all-to-all-done
  16.7 0.6 broadcast.4
  17.3 0.7 reduce.3
  18.0 0.1 reshape.34
  18.1 0.1 copy.29
  18.2 0.1 reshape.35
  18.4 0.7 copy.30.weight_table
  19.1 512.2 %layers.1 = bf16[2,8,16,1280]{3,2,1,0:T(8,128)(2,1)} custom-call(bf16[2,8,16,1280]{3,2,1,0:T(8,128)(2,1)} %bitcast.20, f32[2,1,1280]{2,1,0:T(1,128)} %broadcast_select_fusion.gain, f32[256,16]{1,0:T(8,128)} %copy.30.weight_table, bf16[1,1,2560,768]{3,2,1,0:T(8,128)(2,1)} %gate_hbm.1, bf16[1,1,2560,768]{3,2,1,0:T(8,128)(2,1)} %up_hbm.1, ...), custom_call_target="tpu_custom_call" | custom-call | tf_op jit(solution)/shard_map/layers/pallas_call | solution.py:323
  531.3 1.8 copy.31
  533.0 1.3 reshape.36
  (1 shorter events, 0.0 us)
Async XLA Ops:
  2.9 13.8 %all-to-all-start = ((f32[32,1,128]{2,1,0:T(1,128)}), f32[32,1,128]{2,1,0:T(1,128)S(1)}, u32[]{:S(2)}, u32[]{:S(2)}) async-start(f32[32,1,128]{2,1,0:T(1,128)} %bitcast.5), calls=%async_computation | async-start | bytes 32768 | tf_op jit(solution)/shard_map/all_to_all | solution.py:310

commit v2 on v1

v2 whole, which is shorter than its diff:
```python
import functools

import jax
import jax.numpy as jnp
from jax import lax
from jax.experimental import pallas as pl
from jax.experimental.pallas import tpu as pltpu
from jax.sharding import PartitionSpec as P

MESH = pl.DeviceIdType.MESH
epsilon = 1e-06
SIDE = 4
ROWS = 16
DEPTH = 4
ORDER = (("a", 0), ("b", 1), ("e", 2), ("g", 4), ("f", 3), ("nud", 1))
LOADED = 1


def layer_kernel(
    planes, pieces,
    act, gain, weight_table, gate_hbm, up_hbm, down_hbm,
    out,
    wg, wu, wd, xg, xn, hidden, rs1, rs2, rs3, part_o, part_m, fbuf, obuf,
    w_sem, i_send, i_recv, h_send, x_recv, y_send, y_recv, s_send, s_recv, d_send, r1_recv, e_send, r2_recv,
    f_send, r3_recv, g_send, o_send, o_recv,
):
    block = xg.shape[-1]
    half = 2 * block
    ff = wg.shape[-1]
    groups = SIDE * SIDE // 2
    z = lax.axis_index("pipe")
    e = lax.axis_index("expert")
    core = e % 2
    chip = e // 2
    x, y = chip % SIDE, chip // SIDE
    other = 1 - core
    u = x * other + y * core
    v = y * other + x * core
    su, sv = 2 + (2 * SIDE - 2) * core, 2 * SIDE - (2 * SIDE - 2) * core
    parity = x % 2
    mine = 2 * parity + core

    def dev(u_at, v_at):
        return u_at * su + v_at * sv + core

    sibling = u * su + v * sv + other

    def member(number):
        return (y * SIDE + x - parity + number // 2) * 2 + number % 2

    def wait(sem, ref):
        pltpu.make_async_copy(ref, ref, sem).wait()

    def send(src, dst, send_sem, recv_sem, plane, device):
        pltpu.make_async_remote_copy(
            src_ref=src, dst_ref=dst, send_sem=send_sem, recv_sem=recv_sem,
            device_id=(plane, device), device_id_type=MESH,
        ).start()

    loads = []
    own = pl.ds(pl.multiple_of(core * half, 128), half)
    oth = pl.ds(pl.multiple_of(other * half, 128), half)
    for at, part in ((0, own), (1, oth)):
        rows = pl.ds(at * half, half)
        loads.append(pltpu.make_async_copy(gate_hbm.at[0, 0, part], wg.at[rows], w_sem.at[at]))
        loads.append(pltpu.make_async_copy(up_hbm.at[0, 0, part], wu.at[rows], w_sem.at[2 + at]))
        loads.append(
            pltpu.make_async_copy(down_hbm.at[0, 0, :, part], wd.at[at], w_sem.at[4 + at])
        )
    for load in loads:
        load.start()

    barrier = pltpu.get_barrier_semaphore()

    def greet(plane, device):
        pl.semaphore_signal(barrier, inc=1, device_id=(plane, device), device_id_type=MESH)

    greet(z, sibling)
    greet(z, member(3 - mine))
    for k in range(1, SIDE):
        greet(z, dev(lax.rem(u + k, SIDE), v))
        greet(z, dev(u, lax.rem(v + k, SIDE)))

    @pl.when(z > 0)
    def _():
        for k in range(SIDE):
            greet(z - 1, dev(k, v))

    last = jnp.where(z == planes - 1, 1, 0)
    pl.semaphore_wait(barrier, 2 * SIDE + SIDE * (1 - last))

    def inject(q):
        @pl.when((z == 0) & (4 * q < pieces))
        def _():
            p = 4 * q + mine
            pltpu.make_async_copy(act.at[mine, q], xg.at[p, 0, v, u], i_recv.at[p]).start()
            for k in range(1, 4):
                number = lax.rem(mine + k, 4)
                chip_at = x - parity + number // 2
                core_at = number % 2
                u_at = chip_at * (1 - core_at) + y * core_at
                v_at = y * (1 - core_at) + chip_at * core_at
                send(act.at[number, q], xg.at[p, 0, v_at, u_at], i_send.at[q], i_recv.at[p],
                     z, member(number))

    def stage_h(p):
        @pl.when(z == 0)
        def _():
            wait(i_recv.at[p], obuf.at[p])
            for k in (2, 1, 3):
                send(xg.at[p, 0, v, u], xg.at[p, 0, v, u], h_send.at[p], x_recv.at[p],
                     z, dev(lax.rem(u + k, SIDE), v))

    def relay(p, at):
        send(xg.at[p, 0, at], xg.at[p, 1, :, at], s_send.at[p], s_recv.at[p], z, sibling)

    def stage_a(p):
        @pl.when(z == 0)
        def _():
            wait(x_recv.at[p], xg.at[p, 0, v, 0 : SIDE - 1])

        @pl.when(z > 0)
        def _():
            wait(x_recv.at[p], xg.at[p, 0, v])

        for k in (2, 1, 3):
            send(xg.at[p, 0, v], xg.at[p, 0, v], y_send.at[p], y_recv.at[p, k - 1],
                 z, dev(u, lax.rem(v + k, SIDE)))
        relay(p, v)

    def stage_b(p):
        for k in (1, 3, 2):
            at = lax.rem(v + SIDE - k, SIDE)
            wait(y_recv.at[p, k - 1], xg.at[p, 0, at])
            relay(p, at)

    def place(y_at, x_at):
        return y_at * other + x_at * core, x_at * other + y_at * core

    def stage_n(p):
        wait(s_recv.at[p], xg.at[p, 1])

        def row(y_at, _):
            for j in range(SIDE // 2):
                quarters = []
                for at in range(2):
                    for par in range(2):
                        v_at, u_at = place(y_at, 2 * j + par)
                        quarters.append(xg[p, at, v_at, u_at].astype(jnp.float32))
                square = sum(jnp.sum(t * t, axis=-1, keepdims=True) for t in quarters)
                inverse = lax.rsqrt(square / (2 * half) + epsilon)
                for at, t in enumerate(quarters):
                    cut = slice(at * block, (at + 1) * block)
                    xn[y_at, j, :, cut] = (t * inverse * gain[:, cut]).astype(jnp.bfloat16)
            return 0

        lax.fori_loop(0, SIDE, row, 0)

    def stage_u(p):
        lane = lax.broadcasted_iota(jnp.int32, weight_table.shape, 1)
        scale = jnp.sum(jnp.where(lane == p, weight_table[...], 0.0), axis=1, keepdims=True)
        step = min(256, ff)
        rows = xn[...].reshape(groups * ROWS, 2 * half)
        for n in range(0, ff, step):
            gate_value = jnp.dot(rows, wg[:, n : n + step], preferred_element_type=jnp.float32)
            up_value = jnp.dot(rows, wu[:, n : n + step], preferred_element_type=jnp.float32)
            value = gate_value / (1.0 + jnp.exp(-gate_value)) * up_value * scale
            hidden[:, n : n + step] = value.astype(jnp.bfloat16)

    def stage_d(p):
        slot = p % DEPTH

        @pl.when(p >= DEPTH)
        def _():
            wait(d_send.at[p - DEPTH], part_o.at[slot])
            wait(e_send.at[p - DEPTH], part_m.at[slot, 0 : SIDE - 1])

        for at, part in ((1, part_o), (0, part_m)):
            value = jnp.dot(hidden[...], wd[at], preferred_element_type=jnp.float32)
            value = value.astype(jnp.bfloat16)
            for y_at in range(SIDE):
                for x_at in range(SIDE):
                    v_at, u_at = place(y_at, x_at)
                    top = (y_at * (SIDE // 2) + x_at // 2) * ROWS
                    left = x_at % 2 * block
                    part[slot, v_at, u_at] = value[top : top + ROWS, left : left + block]
            if at == 1:
                for k in range(SIDE):
                    send(part_o.at[slot, k], rs1.at[slot, :, k], d_send.at[p], r1_recv.at[p],
                         z, sibling)

    def stage_e(p):
        slot = p % DEPTH
        wait(r1_recv.at[p], rs1.at[slot])
        for k in (2, 1, 3, 0):
            at = lax.rem(v + k, SIDE)
            value = part_m[slot, at].astype(jnp.float32) + rs1[slot, at].astype(jnp.float32)
            part_m[slot, at] = value.astype(jnp.bfloat16)
            if k:
                send(part_m.at[slot, at], rs2.at[slot, k - 1], e_send.at[p], r2_recv.at[p],
                     z, dev(u, at))

    def stage_f(p):
        slot = p % DEPTH
        wait(r2_recv.at[p], rs2.at[slot])

        @pl.when(p >= DEPTH)
        def _():
            wait(f_send.at[p - DEPTH], fbuf.at[slot, 0 : SIDE - 1])

        for k in (2, 1, 3, 0):
            at = lax.rem(u + k, SIDE)
            value = part_m[slot, v, at].astype(jnp.float32)
            for j in range(SIDE - 1):
                value = value + rs2[slot, j, at].astype(jnp.float32)
            fbuf[slot, at] = value.astype(jnp.bfloat16)
            if k:
                send(fbuf.at[slot, at], rs3.at[p, k - 1], f_send.at[p], r3_recv.at[p],
                     z, dev(at, v))

    def stage_g(p):
        slot = p % DEPTH
        q = p // 4
        wait(r3_recv.at[p], rs3.at[p])
        value = xg[p, 0, v, u].astype(jnp.float32) + fbuf[slot, u].astype(jnp.float32)
        for j in range(SIDE - 1):
            value = value + rs3[p, j].astype(jnp.float32)
        obuf[p] = value.astype(jnp.bfloat16)

        @pl.when(z < planes - 1)
        def _():
            for k in (2, 1, 3, 0):
                send(obuf.at[p], xg.at[p, 0, v, u], g_send.at[p], x_recv.at[p],
                     z + 1, dev(lax.rem(u + k, SIDE), v))

        @pl.when(p % 4 == mine)
        def _():
            pltpu.make_async_copy(obuf.at[p], out.at[mine, q], o_send.at[p]).start()

        @pl.when(p % 4 != mine)
        def _():
            send(obuf.at[p], out.at[mine, q], o_send.at[p], o_recv.at[p], z, member(p % 4))

    inject(0)
    inject(1)
    stage_h(0)

    stages = dict(a=stage_a, b=stage_b, n=stage_n, u=stage_u, d=stage_d, e=stage_e, f=stage_f, g=stage_g)
    ahead = max(lag for _, lag in ORDER)

    def iteration(i, _):
        @pl.when(i == LOADED)
        def _():
            for load in loads:
                load.wait()

        @pl.when(i % 4 == 0)
        def _():
            inject(i // 4 + 2)

        @pl.when(i + 1 < pieces)
        def _():
            stage_h(i + 1)

        for names, lag in ORDER:

            @pl.when((i >= lag) & (i - lag < pieces))
            def _(names=names, lag=lag):
                for name in names:
                    stages[name](i - lag)

        return 0

    lax.fori_loop(0, pieces + ahead, iteration, 0)

    def drain(p, _):
        wait(y_send.at[p], xg.at[p, 0, 0 : SIDE - 1])
        wait(s_send.at[p], xg.at[p, 0])

        @pl.when(p >= pieces - DEPTH)
        def _():
            wait(d_send.at[p], part_o.at[0])
            wait(e_send.at[p], part_m.at[0, 0 : SIDE - 1])
            wait(f_send.at[p], fbuf.at[0, 0 : SIDE - 1])

        @pl.when(z < planes - 1)
        def _():
            wait(g_send.at[p], xg.at[p, 0, v])

        wait(o_send.at[p], obuf.at[p])

        @pl.when(p % 4 == mine)
        def _():
            wait(o_recv.at[p], xg.at[p, 0, 0, 0 : SIDE - 1])

        @pl.when(z == 0)
        def _():
            wait(h_send.at[p], xg.at[p, 0, v, 0 : SIDE - 1])

        @pl.when((z == 0) & (p % 4 == mine))
        def _():
            wait(i_send.at[p // 4], xg.at[p, 0, 0, 0 : SIDE - 1])

        return 0

    lax.fori_loop(0, pieces, drain, 0)


def on_device(
    activations, norm_gain, placement, expert_ids, expert_weights, gate_store, up_store, down_store
):
    planes = lax.axis_size("pipe")
    core = lax.axis_index("expert") % 2
    micro, rows_local, width = activations.shape
    half, block = width // 2, width // 4
    ff = gate_store.shape[-1]
    rows = micro * rows_local
    depth = rows // ROWS
    pieces = 4 * depth
    total = SIDE * SIDE // 2 * ROWS
    bf16 = jnp.bfloat16

    ids = expert_ids.reshape(1, rows, -1)
    weights = expert_weights.reshape(1, rows, -1)
    named = jnp.where(ids == placement[0][:, None, None], weights, 0.0)
    dense = jnp.sum(named, axis=-1)
    table = lax.all_to_all(dense, "expert", split_axis=0, concat_axis=0, tiled=True)
    table = table.reshape(SIDE, SIDE // 2, 4, depth, ROWS).transpose(0, 1, 4, 3, 2)
    table = table.reshape(total, pieces)

    act = activations.reshape(depth, ROWS, 2, 2, block).transpose(3, 2, 0, 1, 4)
    act = act.reshape(4, depth, ROWS, block)
    gain = norm_gain[0].astype(jnp.float32).reshape(2, half)
    gain = jnp.where(core == 0, gain, gain[::-1]).reshape(1, width)

    dma = pltpu.SemaphoreType.DMA
    vmem = pl.BlockSpec(memory_space=pltpu.VMEM)
    hbm = pl.BlockSpec(memory_space=pl.ANY)
    out = pl.pallas_call(
        functools.partial(layer_kernel, planes, pieces),
        out_shape=jax.ShapeDtypeStruct((4, depth, ROWS, block), bf16),
        in_specs=[vmem, vmem, vmem, hbm, hbm, hbm],
        out_specs=vmem,
        scratch_shapes=[
            pltpu.VMEM((width, ff), bf16),
            pltpu.VMEM((width, ff), bf16),
            pltpu.VMEM((2, ff, half), bf16),
            pltpu.VMEM((pieces, 2, SIDE, SIDE, ROWS, block), bf16),
            pltpu.VMEM((SIDE, SIDE // 2, ROWS, width), bf16),
            pltpu.VMEM((total, ff), bf16),
            pltpu.VMEM((DEPTH, SIDE, SIDE, ROWS, block), bf16),
            pltpu.VMEM((DEPTH, SIDE - 1, SIDE, ROWS, block), bf16),
            pltpu.VMEM((pieces, SIDE - 1, ROWS, block), bf16),
            pltpu.VMEM((DEPTH, SIDE, SIDE, ROWS, block), bf16),
            pltpu.VMEM((DEPTH, SIDE, SIDE, ROWS, block), bf16),
            pltpu.VMEM((DEPTH, SIDE, ROWS, block), bf16),
            pltpu.VMEM((pieces, ROWS, block), bf16),
            dma((6,)),
            dma((depth,)),
            *[dma((pieces,))] * 4,
            dma((pieces, SIDE - 1)),
            *[dma((pieces,))] * 11,
        ],
        compiler_params=pltpu.CompilerParams(
            collective_id=0, has_side_effects=True, vmem_limit_bytes=60 * 2**20
        ),
        name="layers",
    )(act, gain, table, gate_store, up_store, down_store)
    out = out.reshape(2, 2, depth, ROWS, block).transpose(2, 3, 1, 0, 4)
    return out.reshape(1, micro, rows_local, width)


def solution(mesh):
    in_specs = (
        P(None, "expert", None),
        P("pipe", None),
        P("pipe", None),
        P("pipe", None, "expert", None),
        P("pipe", None, "expert", None),
        P("pipe", "expert", None, None),
        P("pipe", "expert", None, None),
        P("pipe", "expert", None, None),
    )
    out_specs = P("pipe", None, "expert", None)
    return jax.shard_map(
        on_device, mesh=mesh, in_specs=in_specs, out_specs=out_specs, check_vma=False
    )
```

time: 536 us -> 399 us (0.74)
  Pallas kernels: 512 us -> 377 us
    pallas_call x1, Pallas kernels: 512 us -> 377 us  [on_device(): pl.pallas_call(functools.partial(layer_kernel, planes, pieces), out_shape...]
where the time goes in v2:
time: 399 us
  Pallas kernels  377 us (94%)
  local copies, waits for them, and re-layouts  10.1 us (3%)
  starting transfers between devices  7.93 us (2%)
    pallas_call x1, Pallas kernels, on_device(): pl.pallas_call(functools.partial(layer_kernel, planes, pieces), out_shape...  377 us
  transfers between devices with their start and end apart: 1, of which 1 were waited for; matrix products, arithmetic and copies ran while one was open for 1% of the time, Pallas kernels for 0%

profile of v2, /device:TPU:227, one launch (start us, length us, event | category | flops | bytes accessed | tf_op | source)
XLA Modules:
  0.0 399.0 jit_solution(7805961137212682700)
XLA Ops:
  0.0 0.8 eq.23
  0.8 0.8 broadcast_in_dim.14
  1.5 1.3 select_reduce_fusion
  2.9 7.9 %all-to-all-start = ((f32[32,1,128]{2,1,0:T(1,128)}), f32[32,1,128]{2,1,0:T(1,128)S(1)}, u32[]{:S(2)}, u32[]{:S(2)}) async-start(f32[32,1,128]{2,1,0:T(1,128)} %bitcast.4), calls=%async_computation | async-start | bytes 32768 | tf_op jit(solution)/shard_map/all_to_all | solution.py:327
  10.8 0.7 convert_reduce_fusion
  11.6 0.3 rev.3
  11.9 0.6 copy.30
  12.5 2.1 reshape.33
  14.5 0.9 copy.25
  15.5 1.2 all-to-all-done
  16.7 0.6 broadcast.5
  17.3 0.7 reduce.5
  18.0 0.1 reshape.36
  18.1 0.1 copy.27
  18.2 0.2 reshape.37
  18.4 0.7 copy.28.weight_table
  19.1 376.9 %layers.1 = bf16[4,8,16,640]{3,2,1,0:T(8,128)(2,1)} custom-call(bf16[4,8,16,640]{3,2,1,0:T(8,128)(2,1)} %bitcast.21, f32[1,2560]{1,0:T(1,128)} %bitcast.24, f32[128,32]{1,0:T(8,128)} %copy.28.weight_table, bf16[1,1,2560,768]{3,2,1,0:T(8,128)(2,1)} %gate_hbm.1, bf16[1,1,2560,768]{3,2,1,0:T(8,128)(2,1)} %up_hbm.1, bf16[1,1,768,2560]{3,2,1,0:T(8,128)(2,1)} %down_hbm.1), custom_call_target="tpu_custom_call" | custom-call | tf_op jit(solution)/shard_map/layers/pallas_call | solution.py:339
  396.0 1.8 copy.29
  397.7 1.3 reshape.39
  (2 shorter events, 0.0 us)
Async XLA Ops:
  2.9 13.8 %all-to-all-start = ((f32[32,1,128]{2,1,0:T(1,128)}), f32[32,1,128]{2,1,0:T(1,128)S(1)}, u32[]{:S(2)}, u32[]{:S(2)}) async-start(f32[32,1,128]{2,1,0:T(1,128)} %bitcast.4), calls=%async_computation | async-start | bytes 32768 | tf_op jit(solution)/shard_map/all_to_all | solution.py:327

commit v3 on v2

--- a/solution.py
+++ b/solution.py
@@ -18,10 +18,10 @@
 
 def layer_kernel(
     planes, pieces,
-    act, gain, weight_table, gate_hbm, up_hbm, down_hbm,
+    act, gain_row, ids, weights, slots, gate_hbm, up_hbm, down_hbm,
     out,
-    wg, wu, wd, xg, xn, hidden, rs1, rs2, rs3, part_o, part_m, fbuf, obuf,
-    w_sem, i_send, i_recv, h_send, x_recv, y_send, y_recv, s_send, s_recv, d_send, r1_recv, e_send, r2_recv,
+    gain, told, table, wg, wu, wd, xg, xn, hidden, rs1, rs2, rs3, part_o, part_m, fbuf, obuf,
+    w_sem, t_send, t_recv, i_send, i_recv, h_send, x_recv, y_send, y_recv, s_send, s_recv, d_send, r1_recv, e_send, r2_recv,
     f_send, r3_recv, g_send, o_send, o_recv,
 ):
     block = xg.shape[-1]
@@ -38,6 +38,7 @@
     v = y * other + x * core
     su, sv = 2 + (2 * SIDE - 2) * core, 2 * SIDE - (2 * SIDE - 2) * core
     parity = x % 2
+    per_micro = act.shape[1] // ROWS
     mine = 2 * parity + core
 
     def dev(u_at, v_at):
@@ -75,11 +76,13 @@
     def greet(plane, device):
         pl.semaphore_signal(barrier, inc=1, device_id=(plane, device), device_id_type=MESH)
 
-    greet(z, sibling)
-    greet(z, member(3 - mine))
-    for k in range(1, SIDE):
-        greet(z, dev(lax.rem(u + k, SIDE), v))
-        greet(z, dev(u, lax.rem(v + k, SIDE)))
+    members = 2 * SIDE * SIDE
+
+    def greet_all(k, _):
+        greet(z, lax.rem(e + k, members))
+        return 0
+
+    lax.fori_loop(1, members, greet_all, 0)
 
     @pl.when(z > 0)
     def _():
@@ -87,46 +90,74 @@
             greet(z - 1, dev(k, v))
 
     last = jnp.where(z == planes - 1, 1, 0)
-    pl.semaphore_wait(barrier, 2 * SIDE + SIDE * (1 - last))
+
+    for number in range(members):
+        expert = slots[0, number]
+        value = jnp.zeros((8, ids.shape[1]), jnp.float32)
+        for k in range(ids.shape[0]):
+            value = value + jnp.where(ids[k : k + 1, :] == expert, weights[k : k + 1, :], 0.0)
+        told[number] = value
+    gain[:, 0:half] = gain_row[:, own]
+    gain[:, half:] = gain_row[:, oth]
+
+    pl.semaphore_wait(barrier, members - 1 + SIDE * (1 - last))
+
+    def tell():
+        group = y * (SIDE // 2) + x // 2
+        pltpu.make_async_copy(told.at[e], table.at[mine, group], t_recv).start()
+
+        def one(k, _):
+            device = lax.rem(e + k, members)
+            send(told.at[device], table.at[mine, group], t_send, t_recv, z, device)
+            return 0
+
+        lax.fori_loop(1, members, one, 0)
+
+    def rows_of(ref, q, number):
+        left = pl.multiple_of((number % 2 * 2 + number // 2) * block, 128)
+        top = pl.multiple_of(q % per_micro * ROWS, ROWS)
+        return ref.at[q // per_micro, pl.ds(top, ROWS), pl.ds(left, block)]
 
     def inject(q):
         @pl.when((z == 0) & (4 * q < pieces))
         def _():
             p = 4 * q + mine
-            pltpu.make_async_copy(act.at[mine, q], xg.at[p, 0, v, u], i_recv.at[p]).start()
+            pltpu.make_async_copy(rows_of(act, q, mine), xg.at[p, 0, v, u], i_recv.at[p]).start()
             for k in range(1, 4):
                 number = lax.rem(mine + k, 4)
                 chip_at = x - parity + number // 2
                 core_at = number % 2
                 u_at = chip_at * (1 - core_at) + y * core_at
                 v_at = y * (1 - core_at) + chip_at * core_at
-                send(act.at[number, q], xg.at[p, 0, v_at, u_at], i_send.at[q], i_recv.at[p],
+                send(rows_of(act, q, number), xg.at[p, 0, v_at, u_at], i_send.at[q], i_recv.at[p],
                      z, member(number))
 
     def stage_h(p):
         @pl.when(z == 0)
         def _():
             wait(i_recv.at[p], obuf.at[p])
-            for k in (2, 1, 3):
-                send(xg.at[p, 0, v, u], xg.at[p, 0, v, u], h_send.at[p], x_recv.at[p],
+            for k in (1, 3, 2):
+                send(xg.at[p, 0, v, u], xg.at[p, 0, v, u], h_send.at[p], x_recv.at[p, k],
                      z, dev(lax.rem(u + k, SIDE), v))
 
     def relay(p, at):
         send(xg.at[p, 0, at], xg.at[p, 1, :, at], s_send.at[p], s_recv.at[p], z, sibling)
 
     def stage_a(p):
-        @pl.when(z == 0)
-        def _():
-            wait(x_recv.at[p], xg.at[p, 0, v, 0 : SIDE - 1])
-
-        @pl.when(z > 0)
-        def _():
-            wait(x_recv.at[p], xg.at[p, 0, v])
-
-        for k in (2, 1, 3):
-            send(xg.at[p, 0, v], xg.at[p, 0, v], y_send.at[p], y_recv.at[p, k - 1],
-                 z, dev(u, lax.rem(v + k, SIDE)))
-        relay(p, v)
+        for k in (0, 1, 3, 2):
+            at = lax.rem(u + SIDE - k, SIDE)
+            if k:
+                wait(x_recv.at[p, k], obuf.at[p])
+            else:
+
+                @pl.when(z > 0)
+                def _():
+                    wait(x_recv.at[p, 0], obuf.at[p])
+
+            for j in (2, 1, 3):
+                send(xg.at[p, 0, v, at], xg.at[p, 0, v, at], y_send.at[p], y_recv.at[p, j - 1],
+                     z, dev(u, lax.rem(v + j, SIDE)))
+            send(xg.at[p, 0, v, at], xg.at[p, 1, at, v], s_send.at[p], s_recv.at[p], z, sibling)
 
     def stage_b(p):
         for k in (1, 3, 2):
@@ -157,8 +188,16 @@
         lax.fori_loop(0, SIDE, row, 0)
 
     def stage_u(p):
-        lane = lax.broadcasted_iota(jnp.int32, weight_table.shape, 1)
-        scale = jnp.sum(jnp.where(lane == p, weight_table[...], 0.0), axis=1, keepdims=True)
+        @pl.when(p == 0)
+        def _():
+            wait(t_recv, table)
+
+        named = table[p % 4]
+        named = jnp.concatenate([named, named], axis=1)
+        token = p // 4 * ROWS + lax.broadcasted_iota(jnp.int32, named.shape, 1)
+        lane = lax.broadcasted_iota(jnp.int32, named.shape, 2)
+        scale = jnp.sum(jnp.where(lane == token, named, 0.0), axis=2, keepdims=True)
+        scale = scale.reshape(groups * ROWS, 1)
         step = min(256, ff)
         rows = xn[...].reshape(groups * ROWS, 2 * half)
         for n in range(0, ff, step):
@@ -229,19 +268,20 @@
 
         @pl.when(z < planes - 1)
         def _():
-            for k in (2, 1, 3, 0):
-                send(obuf.at[p], xg.at[p, 0, v, u], g_send.at[p], x_recv.at[p],
+            for k in (0, 1, 3, 2):
+                send(obuf.at[p], xg.at[p, 0, v, u], g_send.at[p], x_recv.at[p, k],
                      z + 1, dev(lax.rem(u + k, SIDE), v))
 
         @pl.when(p % 4 == mine)
         def _():
-            pltpu.make_async_copy(obuf.at[p], out.at[mine, q], o_send.at[p]).start()
+            pltpu.make_async_copy(obuf.at[p], rows_of(out, q, mine), o_send.at[p]).start()
 
         @pl.when(p % 4 != mine)
         def _():
-            send(obuf.at[p], out.at[mine, q], o_send.at[p], o_recv.at[p], z, member(p % 4))
+            send(obuf.at[p], rows_of(out, q, mine), o_send.at[p], o_recv.at[p], z, member(p % 4))
 
     inject(0)
+    tell()
     inject(1)
     stage_h(0)
 
@@ -304,13 +344,14 @@
         return 0
 
     lax.fori_loop(0, pieces, drain, 0)
+    wait(t_send, told.at[0 : members - 1])
 
 
 def on_device(
     activations, norm_gain, placement, expert_ids, expert_weights, gate_store, up_store, down_store
 ):
     planes = lax.axis_size("pipe")
-    core = lax.axis_index("expert") % 2
+    members = lax.axis_size("expert")
     micro, rows_local, width = activations.shape
     half, block = width // 2, width // 4
     ff = gate_store.shape[-1]
@@ -319,29 +360,22 @@
     pieces = 4 * depth
     total = SIDE * SIDE // 2 * ROWS
     bf16 = jnp.bfloat16
-
-    ids = expert_ids.reshape(1, rows, -1)
-    weights = expert_weights.reshape(1, rows, -1)
-    named = jnp.where(ids == placement[0][:, None, None], weights, 0.0)
-    dense = jnp.sum(named, axis=-1)
-    table = lax.all_to_all(dense, "expert", split_axis=0, concat_axis=0, tiled=True)
-    table = table.reshape(SIDE, SIDE // 2, 4, depth, ROWS).transpose(0, 1, 4, 3, 2)
-    table = table.reshape(total, pieces)
-
-    act = activations.reshape(depth, ROWS, 2, 2, block).transpose(3, 2, 0, 1, 4)
-    act = act.reshape(4, depth, ROWS, block)
-    gain = norm_gain[0].astype(jnp.float32).reshape(2, half)
-    gain = jnp.where(core == 0, gain, gain[::-1]).reshape(1, width)
+    ids = expert_ids.reshape(rows, -1).T
+    weights = expert_weights.reshape(rows, -1).T
 
     dma = pltpu.SemaphoreType.DMA
     vmem = pl.BlockSpec(memory_space=pltpu.VMEM)
+    smem = pl.BlockSpec(memory_space=pltpu.SMEM)
     hbm = pl.BlockSpec(memory_space=pl.ANY)
     out = pl.pallas_call(
         functools.partial(layer_kernel, planes, pieces),
-        out_shape=jax.ShapeDtypeStruct((4, depth, ROWS, block), bf16),
-        in_specs=[vmem, vmem, vmem, hbm, hbm, hbm],
+        out_shape=jax.ShapeDtypeStruct((micro, rows_local, width), bf16),
+        in_specs=[hbm, vmem, vmem, vmem, smem, hbm, hbm, hbm],
         out_specs=vmem,
         scratch_shapes=[
+            pltpu.VMEM((1, width), jnp.float32),
+            pltpu.VMEM((members, 8, rows), jnp.float32),
+            pltpu.VMEM((4, SIDE * SIDE // 2, 8, rows), jnp.float32),
             pltpu.VMEM((width, ff), bf16),
             pltpu.VMEM((width, ff), bf16),
             pltpu.VMEM((2, ff, half), bf16),
@@ -356,8 +390,13 @@
             pltpu.VMEM((DEPTH, SIDE, ROWS, block), bf16),
             pltpu.VMEM((pieces, ROWS, block), bf16),
             dma((6,)),
+            dma,
+            dma,
             dma((depth,)),
-            *[dma((pieces,))] * 4,
+            dma((pieces,)),
+            dma((pieces,)),
+            dma((pieces, SIDE)),
+            dma((pieces,)),
             dma((pieces, SIDE - 1)),
             *[dma((pieces,))] * 11,
         ],
@@ -365,9 +404,8 @@
             collective_id=0, has_side_effects=True, vmem_limit_bytes=60 * 2**20
         ),
         name="layers",
-    )(act, gain, table, gate_store, up_store, down_store)
-    out = out.reshape(2, 2, depth, ROWS, block).transpose(2, 3, 1, 0, 4)
-    return out.reshape(1, micro, rows_local, width)
+    )(activations, norm_gain.astype(jnp.float32), ids, weights, placement, gate_store, up_store, down_store)
+    return out[None]
 
 
 def solution(mesh):

time: 399 us -> 384 us (0.962)
  starting transfers between devices: 7.93 us -> 0 us
  local copies, waits for them, and re-layouts: 10.1 us -> 4.67 us
    all_to_all x1 -> x0, starting transfers between devices: 7.93 us -> none  [on_device(): lax.all_to_all(dense, 'expert', split_axis=0, concat_axis=0, tiled=True)]
  transfers between devices with their start and end apart: 1 -> 0, of which waited for: 1 -> 0; matrix products, arithmetic and copies ran while one was open for 1% -> 0% of each run, Pallas kernels for 0% -> 0%
where the time goes in v3:
time: 384 us; the launch traced here: 383 us
  Pallas kernels  377 us (98%)
  local copies, waits for them, and re-layouts  4.67 us (1%)
    pallas_call x1, Pallas kernels, on_device(): pl.pallas_call(functools.partial(layer_kernel, planes, pieces), out_shape...  377 us

profile of v3, /device:TPU:227, one launch (start us, length us, event | category | flops | bytes accessed | tf_op | source)
XLA Modules:
  0.0 383.2 jit_solution(15554133444807636781)
XLA Ops:
  0.0 1.3 reshape.6
  1.3 1.4 reshape.7
  2.7 1.3 convert_element_type.3.gain_row
  4.0 377.3 %layers.1 = bf16[2,64,2560]{2,1,0:T(8,128)(2,1)} custom-call(bf16[2,64,2560]{2,1,0:T(8,128)(2,1)} %act.1, f32[1,2560]{1,0:T(1,128)} %convert_element_type.3.gain_row, s32[6,128]{1,0:T(8,128)} %bitcast.8, f32[6,128]{1,0:T(8,128)} %bitcast.9, s32[1,32]{1,0:T(1,128)} %slots.1, bf16[1,1,2560,768]{3,2,1,0:T(8,128)(2,1)} %gate_hbm.1, ...), custom_call_target="tpu_custom_call" | custom-call | tf_op jit(solution)/shard_map/layers/pallas_call | solution.py:370
  381.3 2.0 copy.10

commit v4 on v3

--- a/solution.py
+++ b/solution.py
@@ -224,31 +224,33 @@
                     left = x_at % 2 * block
                     part[slot, v_at, u_at] = value[top : top + ROWS, left : left + block]
             if at == 1:
-                for k in range(SIDE):
-                    send(part_o.at[slot, k], rs1.at[slot, :, k], d_send.at[p], r1_recv.at[p],
+                for k in (2, 1, 3, 0):
+                    to = lax.rem(v + k, SIDE)
+                    send(part_o.at[slot, to], rs1.at[slot, :, to], d_send.at[p], r1_recv.at[p, k],
                          z, sibling)
 
     def stage_e(p):
         slot = p % DEPTH
-        wait(r1_recv.at[p], rs1.at[slot])
-        for k in (2, 1, 3, 0):
-            at = lax.rem(v + k, SIDE)
-            value = part_m[slot, at].astype(jnp.float32) + rs1[slot, at].astype(jnp.float32)
-            part_m[slot, at] = value.astype(jnp.bfloat16)
-            if k:
-                send(part_m.at[slot, at], rs2.at[slot, k - 1], e_send.at[p], r2_recv.at[p],
-                     z, dev(u, at))
+        for j in (2, 1, 3, 0):
+            to = lax.rem(u + j, SIDE)
+            wait(r1_recv.at[p, j], rs1.at[slot, :, to])
+            for k in (2, 1, 3, 0):
+                at = lax.rem(v + k, SIDE)
+                value = part_m[slot, at, to].astype(jnp.float32) + rs1[slot, at, to].astype(jnp.float32)
+                part_m[slot, at, to] = value.astype(jnp.bfloat16)
+                if k:
+                    send(part_m.at[slot, at, to], rs2.at[slot, k - 1, to], e_send.at[p],
+                         r2_recv.at[p, j], z, dev(u, at))
 
     def stage_f(p):
         slot = p % DEPTH
-        wait(r2_recv.at[p], rs2.at[slot])
-
         @pl.when(p >= DEPTH)
         def _():
             wait(f_send.at[p - DEPTH], fbuf.at[slot, 0 : SIDE - 1])
 
         for k in (2, 1, 3, 0):
             at = lax.rem(u + k, SIDE)
+            wait(r2_recv.at[p, k], rs2.at[slot, :, at])
             value = part_m[slot, v, at].astype(jnp.float32)
             for j in range(SIDE - 1):
                 value = value + rs2[slot, j, at].astype(jnp.float32)
@@ -398,7 +400,11 @@
             dma((pieces, SIDE)),
             dma((pieces,)),
             dma((pieces, SIDE - 1)),
-            *[dma((pieces,))] * 11,
+            *[dma((pieces,))] * 3,
+            dma((pieces, SIDE)),
+            dma((pieces,)),
+            dma((pieces, SIDE)),
+            *[dma((pieces,))] * 5,
         ],
         compiler_params=pltpu.CompilerParams(
             collective_id=0, has_side_effects=True, vmem_limit_bytes=60 * 2**20

time: 384 us -> 384 us (level)
  no operation moved by 1% of the time
where the time goes in v4:
time: 384 us
  Pallas kernels  378 us (98%)
  local copies, waits for them, and re-layouts  4.67 us (1%)
    pallas_call x1, Pallas kernels, on_device(): pl.pallas_call(functools.partial(layer_kernel, planes, pieces), out_shape...  378 us

profile of v4, /device:TPU:227, one launch (start us, length us, event | category | flops | bytes accessed | tf_op | source)
XLA Modules:
  0.0 383.9 jit_solution(4562531847102314106)
XLA Ops:
  0.0 1.3 reshape.6
  1.3 1.4 reshape.7
  2.7 1.3 convert_element_type.3.gain_row
  4.0 377.9 %layers.1 = bf16[2,64,2560]{2,1,0:T(8,128)(2,1)} custom-call(bf16[2,64,2560]{2,1,0:T(8,128)(2,1)} %act.1, f32[1,2560]{1,0:T(1,128)} %convert_element_type.3.gain_row, s32[6,128]{1,0:T(8,128)} %bitcast.8, f32[6,128]{1,0:T(8,128)} %bitcast.9, s32[1,32]{1,0:T(1,128)} %slots.1, bf16[1,1,2560,768]{3,2,1,0:T(8,128)(2,1)} %gate_hbm.1, ...), custom_call_target="tpu_custom_call" | custom-call | tf_op jit(solution)/shard_map/layers/pallas_call | solution.py:372
  381.9 2.0 copy.10
